TPU v7x, 32 devices: a whole 2x2x4 slice. The times are simulated.
32 devices in a mesh: dp: 8 (over z, x), rep: 4 (over y, core).
Axes of the slice: x: 2, y: 2, z: 4, core: 2. Of those that a mesh axis runs over, the one named last changes fastest.
Arguments:
- tokens_in: bfloat16 [8192, 768], P(('dp', 'rep')), may hold values from -7 to 7
- boxes: int32 [2, 8192], P(None, ('dp', 'rep')), may hold values from 0 to 999
- page_lengths: int32 [32, 8], P(('dp', 'rep')), may hold values from 1 to 64, 256 in all within a row
- cotangent: bfloat16 [8192, 768], P(('dp', 'rep')), may hold values from -6 to 6
- w_qkv: bfloat16 [768, 2304], P(('dp', 'rep')), may hold values from -0.21875 to 0.21875
- w_out: bfloat16 [768, 768], P(('dp', 'rep')), may hold values from -0.875 to 0.875
- w_pos: bfloat16 [768, 768], P(('dp', 'rep')), may hold values from -0.21875 to 0.21875
- gain_attn: bfloat16 [768], P(('dp', 'rep')), may hold values from 0.5 to 1.5
- bias_attn: bfloat16 [768], P(('dp', 'rep')), may hold values from -1.1953125 to 1.1953125
- w_up: bfloat16 [768, 3072], P(('dp', 'rep')), may hold values from -0.21875 to 0.21875
- w_down: bfloat16 [3072, 768], P(('dp', 'rep')), may hold values from -0.109375 to 0.109375
- gain_ffn: bfloat16 [768], P(('dp', 'rep')), may hold values from 0.5 to 1.5
- bias_ffn: bfloat16 [768], P(('dp', 'rep')), may hold values from -1.1953125 to 1.1953125
Outputs:
- output: bfloat16 [8192, 768], P(('dp', 'rep'))
- grad_tokens: float32 [8192, 768], P(('dp', 'rep'))
- rms: float32 [3], replicated
- grad_w_qkv: float32 [768, 2304], P(('dp', 'rep'))
- grad_w_out: float32 [768, 768], P(('dp', 'rep'))
- grad_w_pos: float32 [768, 768], P(('dp', 'rep'))
- grad_gain_attn: float32 [768], P(('dp', 'rep'))
- grad_bias_attn: float32 [768], P(('dp', 'rep'))
- grad_w_up: float32 [768, 3072], P(('dp', 'rep'))
- grad_w_down: float32 [3072, 768], P(('dp', 'rep'))
- grad_gain_ffn: float32 [768], P(('dp', 'rep'))
- grad_bias_ffn: float32 [768], P(('dp', 'rep'))
All inputs are finite; a program needn't handle non-finite values.
Results may differ from a plain program's by a relative error of at most 0.018.
Values may be sent and summed in bfloat16 or wider, within the bound.
No kernel may reach another device: no remote copies, remote signals or barrier semaphores. Data moves between devices by JAX's collectives and lax.ppermute only.
A program may use at most 192 MiB of HBM per device.

v0:
```python
from functools import partial
import math

import jax
import jax.numpy as jnp
from jax import lax
from jax.sharding import PartitionSpec as P

HEADS = 12
FREQS = 192


epsilon = 1e-05
masked_value = -1e30


def sinusoid_parts(boxes, freq_count):
    steps_f = jnp.arange(freq_count, dtype=jnp.float32)
    rates = jnp.exp(steps_f * (-math.log(10000.0) / freq_count))
    angles = boxes.astype(jnp.float32)[:, :, None] * rates[None, None, :]
    return (jnp.sin(angles), jnp.cos(angles))


def token_features(sines, cosines):
    stacked = jnp.stack([sines, cosines], axis=1)
    tok_count = sines.shape[1]
    return jnp.transpose(stacked, (2, 0, 1, 3)).reshape(tok_count, -1)


def rotate(coeff, sin_tok, cos_tok):
    tok_count, head_count, pos_width = coeff.shape
    parts = coeff.reshape(tok_count, head_count, 2, 2, pos_width // 4)
    along_sin = parts[:, :, :, 0, :]
    along_cos = parts[:, :, :, 1, :]
    first = along_cos * sin_tok - along_sin * cos_tok
    second = along_sin * sin_tok + along_cos * cos_tok
    return jnp.stack([first, second], axis=3).reshape(tok_count, head_count, pos_width)


def rotate_back(grads, sin_tok, cos_tok):
    tok_count, head_count, pos_width = grads.shape
    parts = grads.reshape(tok_count, head_count, 2, 2, pos_width // 4)
    first = parts[:, :, :, 0, :]
    second = parts[:, :, :, 1, :]
    grad_sin = second * sin_tok - first * cos_tok
    grad_cos = first * sin_tok + second * cos_tok
    return jnp.stack([grad_sin, grad_cos], axis=3).reshape(tok_count, head_count, pos_width)


def segment_ids(page_lengths, row_len):
    ends = jnp.cumsum(page_lengths, axis=1)
    places = jnp.arange(row_len, dtype=jnp.int32)
    return jnp.sum((places[None, :, None] >= ends[:, None, :]).astype(jnp.int32), axis=2)


def norm_forward(values, gain, bias):
    centered = values - jnp.mean(values, axis=-1, keepdims=True)
    inv_std = lax.rsqrt(jnp.mean(centered * centered, axis=-1, keepdims=True) + epsilon)
    normed_vals = centered * inv_std
    return (normed_vals * gain + bias, normed_vals, inv_std)


def norm_backward(grad, normed_vals, inv_std, gain):
    grad_normed = grad * gain
    centered_grad = grad_normed - jnp.mean(grad_normed, axis=-1, keepdims=True)
    grad_values = inv_std * (
        centered_grad - normed_vals * jnp.mean(grad_normed * normed_vals, axis=-1, keepdims=True)
    )
    return (grad_values, jnp.sum(grad * normed_vals, axis=0), jnp.sum(grad, axis=0))


def gelu_exact(values):
    return jax.nn.gelu(values, approximate=False)


def fetch_weights(w_qkv, w_out, w_pos, w_up, w_down, gain_attn, bias_attn, gain_ffn, bias_ffn):
    inner = (
        lax.all_gather(w_qkv, "rep", axis=0, tiled=True),
        lax.all_gather(w_out, "rep", axis=0, tiled=True),
        lax.all_gather(w_pos, "rep", axis=0, tiled=True),
        lax.all_gather(w_up, "rep", axis=0, tiled=True),
        lax.all_gather(w_down, "rep", axis=0, tiled=True),
        lax.all_gather(gain_attn, "rep", axis=0, tiled=True),
        lax.all_gather(bias_attn, "rep", axis=0, tiled=True),
        lax.all_gather(gain_ffn, "rep", axis=0, tiled=True),
        lax.all_gather(bias_ffn, "rep", axis=0, tiled=True),
    )
    in_qkv, in_out, in_pos, in_up, in_down, in_gain_attn, in_bias_attn, in_gain_ffn, in_bias_ffn = (
        inner
    )
    return (
        lax.all_gather(in_qkv, "dp", axis=0, tiled=True),
        lax.all_gather(in_out, "dp", axis=0, tiled=True),
        lax.all_gather(in_pos, "dp", axis=0, tiled=True),
        lax.all_gather(in_up, "dp", axis=0, tiled=True),
        lax.all_gather(in_down, "dp", axis=0, tiled=True),
        lax.all_gather(in_gain_attn, "dp", axis=0, tiled=True),
        lax.all_gather(in_bias_attn, "dp", axis=0, tiled=True),
        lax.all_gather(in_gain_ffn, "dp", axis=0, tiled=True),
        lax.all_gather(in_bias_ffn, "dp", axis=0, tiled=True),
    )


def row_scores(query, key, query_pos, key_pos, feats, segment, scale):
    plain = jnp.einsum("ihd,jhd->hij", query, key, preferred_element_type=jnp.float32)
    to_pos = jnp.einsum("ihp,jp->hij", query_pos, feats, preferred_element_type=jnp.float32)
    from_pos = jnp.einsum("ip,jhp->hij", feats, key_pos, preferred_element_type=jnp.float32)
    raw = (plain + to_pos + from_pos) * scale
    same = segment[:, None] == segment[None, :]
    return jnp.where(same[None], raw, masked_value)


def attend_forward(items, scale):
    query, key, value, query_pos, key_pos, feats, segment = items
    scores = row_scores(query, key, query_pos, key_pos, feats, segment, scale)
    top = jnp.max(scores, axis=-1, keepdims=True)
    expo = jnp.exp(scores - top)
    total = jnp.sum(expo, axis=-1, keepdims=True)
    probs = (expo / total).astype(jnp.bfloat16)
    mixed = jnp.einsum("hij,jhd->ihd", probs, value, preferred_element_type=jnp.float32)
    return (mixed, (top + jnp.log(total))[:, :, 0])


def attend_backward(items, scale):
    query, key, value, query_pos, key_pos, feats, segment, log_total, grad_mixed = items
    scores = row_scores(query, key, query_pos, key_pos, feats, segment, scale)
    probs = jnp.exp(scores - log_total[:, :, None])
    grad_value = jnp.einsum(
        "hij,ihd->jhd", probs.astype(jnp.bfloat16), grad_mixed, preferred_element_type=jnp.float32
    )
    grad_probs = jnp.einsum("ihd,jhd->hij", grad_mixed, value, preferred_element_type=jnp.float32)
    row_inner = jnp.sum(probs * grad_probs, axis=-1, keepdims=True)
    grad_scores = (probs * (grad_probs - row_inner)).astype(jnp.bfloat16)
    grad_query = (
        jnp.einsum("hij,jhd->ihd", grad_scores, key, preferred_element_type=jnp.float32) * scale
    )
    grad_key = (
        jnp.einsum("hij,ihd->jhd", grad_scores, query, preferred_element_type=jnp.float32) * scale
    )
    grad_query_pos = (
        jnp.einsum("hij,jp->ihp", grad_scores, feats, preferred_element_type=jnp.float32) * scale
    )
    grad_key_pos = (
        jnp.einsum("hij,ip->jhp", grad_scores, feats, preferred_element_type=jnp.float32) * scale
    )
    return (grad_query, grad_key, grad_value, grad_query_pos, grad_key_pos)


def body(
    tokens_in,
    boxes,
    page_lengths,
    cotangent,
    w_qkv,
    w_out,
    w_pos,
    gain_attn,
    bias_attn,
    w_up,
    w_down,
    gain_ffn,
    bias_ffn,
):
    tok_count, width = tokens_in.shape
    row_count = page_lengths.shape[0]
    row_len = tok_count // row_count
    head_dim = width // HEADS
    pos_width = 4 * FREQS
    scale = head_dim ** (-0.5)

    def by_rows(values):
        return values.reshape((row_count, row_len) + values.shape[1:])

    (
        full_qkv,
        full_out,
        full_pos,
        full_up,
        full_down,
        full_gain_attn,
        full_bias_attn,
        full_gain_ffn,
        full_bias_ffn,
    ) = fetch_weights(w_qkv, w_out, w_pos, w_up, w_down, gain_attn, bias_attn, gain_ffn, bias_ffn)
    sines, cosines = sinusoid_parts(boxes, FREQS)
    sin_tok = jnp.transpose(sines, (1, 0, 2))[:, None]
    cos_tok = jnp.transpose(cosines, (1, 0, 2))[:, None]
    feats = token_features(sines, cosines).astype(jnp.bfloat16)
    segments = segment_ids(page_lengths, row_len)
    qkv = jnp.dot(tokens_in, full_qkv, preferred_element_type=jnp.float32).astype(jnp.bfloat16)
    qkv = qkv.reshape(tok_count, 3, HEADS, head_dim)
    query = qkv[:, 0]
    key = qkv[:, 1]
    value = qkv[:, 2]
    pos_weights = full_pos.reshape(pos_width, HEADS, head_dim)
    query_coeff = jnp.einsum("thd,phd->thp", query, pos_weights, preferred_element_type=jnp.float32)
    key_coeff = jnp.einsum("thd,phd->thp", key, pos_weights, preferred_element_type=jnp.float32)
    query_pos = rotate(query_coeff, sin_tok, cos_tok).astype(jnp.bfloat16)
    key_pos = rotate(key_coeff, sin_tok, cos_tok).astype(jnp.bfloat16)
    row_items = (
        by_rows(query),
        by_rows(key),
        by_rows(value),
        by_rows(query_pos),
        by_rows(key_pos),
        by_rows(feats),
        segments,
    )
    mixed, log_total = lax.map(partial(attend_forward, scale=scale), row_items)
    context = mixed.reshape(tok_count, width).astype(jnp.bfloat16)
    attn_out = jnp.dot(context, full_out, preferred_element_type=jnp.float32)
    tokens_f = tokens_in.astype(jnp.float32)
    resid_sum = tokens_f + attn_out
    normed_one, normed_vals_one, inv_std_one = norm_forward(
        resid_sum, full_gain_attn.astype(jnp.float32), full_bias_attn.astype(jnp.float32)
    )
    normed_low = normed_one.astype(jnp.bfloat16)
    pre_act = jnp.dot(normed_low, full_up, preferred_element_type=jnp.float32)
    act_low = gelu_exact(pre_act).astype(jnp.bfloat16)
    ffn_out = jnp.dot(act_low, full_down, preferred_element_type=jnp.float32)
    output, normed_vals_two, inv_std_two = norm_forward(
        normed_one + ffn_out, full_gain_ffn.astype(jnp.float32), full_bias_ffn.astype(jnp.float32)
    )
    sum_tokens, sum_attn, sum_resid = lax.psum(
        (
            jnp.sum(tokens_f * tokens_f),
            jnp.sum(attn_out * attn_out),
            jnp.sum(resid_sum * resid_sum),
        ),
        ("dp", "rep"),
    )
    entry_count = tok_count * width * lax.axis_size("dp") * lax.axis_size("rep")
    rms_values = jnp.sqrt(jnp.stack([sum_tokens, sum_attn, sum_resid]) / entry_count)
    (
        back_qkv,
        back_out,
        back_pos,
        back_up,
        back_down,
        back_gain_attn,
        back_bias_attn,
        back_gain_ffn,
        back_bias_ffn,
    ) = fetch_weights(w_qkv, w_out, w_pos, w_up, w_down, gain_attn, bias_attn, gain_ffn, bias_ffn)
    back_pos_heads = back_pos.reshape(pos_width, HEADS, head_dim)
    grad_resid_two, grad_gain_ffn, grad_bias_ffn = norm_backward(
        cotangent.astype(jnp.float32),
        normed_vals_two,
        inv_std_two,
        back_gain_ffn.astype(jnp.float32),
    )
    grad_ffn_low = grad_resid_two.astype(jnp.bfloat16)
    grad_w_down = jnp.einsum("tf,td->fd", act_low, grad_ffn_low, preferred_element_type=jnp.float32)
    grad_act = jnp.einsum("td,fd->tf", grad_ffn_low, back_down, preferred_element_type=jnp.float32)
    unused_value, gelu_pull = jax.vjp(gelu_exact, pre_act)
    grad_pre = gelu_pull(grad_act)[0].astype(jnp.bfloat16)
    grad_w_up = jnp.einsum("td,tf->df", normed_low, grad_pre, preferred_element_type=jnp.float32)
    grad_normed = grad_resid_two + jnp.einsum(
        "tf,df->td", grad_pre, back_up, preferred_element_type=jnp.float32
    )
    grad_resid_one, grad_gain_attn, grad_bias_attn = norm_backward(
        grad_normed, normed_vals_one, inv_std_one, back_gain_attn.astype(jnp.float32)
    )
    grad_attn_low = grad_resid_one.astype(jnp.bfloat16)
    grad_w_out = jnp.einsum("tc,td->cd", context, grad_attn_low, preferred_element_type=jnp.float32)
    grad_context = jnp.einsum(
        "td,cd->tc", grad_attn_low, back_out, preferred_element_type=jnp.float32
    ).astype(jnp.bfloat16)
    back_items = row_items + (log_total, by_rows(grad_context.reshape(tok_count, HEADS, head_dim)))
    grad_query, grad_key, grad_value, grad_query_pos, grad_key_pos = lax.map(
        partial(attend_backward, scale=scale), back_items
    )
    grad_query_coeff = rotate_back(
        grad_query_pos.reshape(tok_count, HEADS, pos_width), sin_tok, cos_tok
    ).astype(jnp.bfloat16)
    grad_key_coeff = rotate_back(
        grad_key_pos.reshape(tok_count, HEADS, pos_width), sin_tok, cos_tok
    ).astype(jnp.bfloat16)
    grad_w_pos = jnp.einsum(
        "thp,thd->phd", grad_query_coeff, query, preferred_element_type=jnp.float32
    )
    grad_w_pos = (
        grad_w_pos
        + jnp.einsum("thp,thd->phd", grad_key_coeff, key, preferred_element_type=jnp.float32)
    ).reshape(pos_width, width)
    grad_query = grad_query.reshape(tok_count, HEADS, head_dim) + jnp.einsum(
        "thp,phd->thd", grad_query_coeff, back_pos_heads, preferred_element_type=jnp.float32
    )
    grad_key = grad_key.reshape(tok_count, HEADS, head_dim) + jnp.einsum(
        "thp,phd->thd", grad_key_coeff, back_pos_heads, preferred_element_type=jnp.float32
    )
    grad_value = grad_value.reshape(tok_count, HEADS, head_dim)
    grad_qkv = (
        jnp.stack([grad_query, grad_key, grad_value], axis=1)
        .reshape(tok_count, 3 * width)
        .astype(jnp.bfloat16)
    )
    grad_w_qkv = jnp.einsum("td,te->de", tokens_in, grad_qkv, preferred_element_type=jnp.float32)
    grad_tokens = grad_resid_one + jnp.einsum(
        "te,de->td", grad_qkv, back_qkv, preferred_element_type=jnp.float32
    )
    outer = (
        lax.psum_scatter(grad_w_qkv, "dp", scatter_dimension=0, tiled=True),
        lax.psum_scatter(grad_w_out, "dp", scatter_dimension=0, tiled=True),
        lax.psum_scatter(grad_w_pos, "dp", scatter_dimension=0, tiled=True),
        lax.psum_scatter(grad_w_up, "dp", scatter_dimension=0, tiled=True),
        lax.psum_scatter(grad_w_down, "dp", scatter_dimension=0, tiled=True),
        lax.psum_scatter(grad_gain_attn, "dp", scatter_dimension=0, tiled=True),
        lax.psum_scatter(grad_bias_attn, "dp", scatter_dimension=0, tiled=True),
        lax.psum_scatter(grad_gain_ffn, "dp", scatter_dimension=0, tiled=True),
        lax.psum_scatter(grad_bias_ffn, "dp", scatter_dimension=0, tiled=True),
    )
    (
        part_qkv,
        part_out,
        part_pos,
        part_up,
        part_down,
        part_gain_attn,
        part_bias_attn,
        part_gain_ffn,
        part_bias_ffn,
    ) = outer
    (
        sum_qkv,
        sum_out,
        sum_pos,
        sum_up,
        sum_down,
        sum_gain_attn,
        sum_bias_attn,
        sum_gain_ffn,
        sum_bias_ffn,
    ) = (
        lax.psum_scatter(
            part_qkv.astype(jnp.bfloat16), "rep", scatter_dimension=0, tiled=True
        ).astype(jnp.float32),
        lax.psum_scatter(
            part_out.astype(jnp.bfloat16), "rep", scatter_dimension=0, tiled=True
        ).astype(jnp.float32),
        lax.psum_scatter(
            part_pos.astype(jnp.bfloat16), "rep", scatter_dimension=0, tiled=True
        ).astype(jnp.float32),
        lax.psum_scatter(
            part_up.astype(jnp.bfloat16), "rep", scatter_dimension=0, tiled=True
        ).astype(jnp.float32),
        lax.psum_scatter(
            part_down.astype(jnp.bfloat16), "rep", scatter_dimension=0, tiled=True
        ).astype(jnp.float32),
        lax.psum_scatter(
            part_gain_attn.astype(jnp.bfloat16), "rep", scatter_dimension=0, tiled=True
        ).astype(jnp.float32),
        lax.psum_scatter(
            part_bias_attn.astype(jnp.bfloat16), "rep", scatter_dimension=0, tiled=True
        ).astype(jnp.float32),
        lax.psum_scatter(
            part_gain_ffn.astype(jnp.bfloat16), "rep", scatter_dimension=0, tiled=True
        ).astype(jnp.float32),
        lax.psum_scatter(
            part_bias_ffn.astype(jnp.bfloat16), "rep", scatter_dimension=0, tiled=True
        ).astype(jnp.float32),
    )
    return (
        output.astype(jnp.bfloat16),
        grad_tokens,
        rms_values,
        sum_qkv,
        sum_out,
        sum_pos,
        sum_gain_attn,
        sum_bias_attn,
        sum_up,
        sum_down,
        sum_gain_ffn,
        sum_bias_ffn,
    )


def solution(mesh):
    in_specs = (
        P(("dp", "rep"), None),
        P(None, ("dp", "rep")),
        P(("dp", "rep"), None),
        P(("dp", "rep"), None),
        P(("dp", "rep"), None),
        P(("dp", "rep"), None),
        P(("dp", "rep"), None),
        P(("dp", "rep")),
        P(("dp", "rep")),
        P(("dp", "rep"), None),
        P(("dp", "rep"), None),
        P(("dp", "rep")),
        P(("dp", "rep")),
    )
    out_specs = (
        P(("dp", "rep"), None),
        P(("dp", "rep"), None),
        P(),
        P(("dp", "rep"), None),
        P(("dp", "rep"), None),
        P(("dp", "rep"), None),
        P(("dp", "rep")),
        P(("dp", "rep")),
        P(("dp", "rep"), None),
        P(("dp", "rep"), None),
        P(("dp", "rep")),
        P(("dp", "rep")),
    )
    return jax.shard_map(body, mesh=mesh, in_specs=in_specs, out_specs=out_specs, check_vma=False)
```

profile of v0, /device:TPU:0, one launch (start us, length us, event | category | flops | bytes accessed | tf_op | source)
XLA Modules:
  0.0 1118.0 jit_solution(11296031351093726436)
XLA Ops:
  7.3 8.4 all_gather.70
  15.8 7.9 all_gather.68
  23.8 6.9 all_gather.72
  30.8 8.8 all_gather.78
  39.7 9.6 all_gather.80
  63.6 22.6 %all-reduce.18 = (bf16[768]{0:T(1024)(128)(2,1)S(1)}, bf16[768]{0:T(1024)(128)(2,1)S(1)}, bf16[768]{0:T(1024)(128)(2,1)S(1)}, bf16[768]{0:T(1024)(128)(2,1)S(1)}) all-reduce(bf16[768]{0:T(1024)(128)(2,1)S(1)} %dynamic-update-slice.3, bf16[768]{0:T(1024)(128)(2,1)S(1)} %dynamic-update-slice.1, ...), channel_id=1, replica_groups=mesh['dp'=8,'rep'=4] {'dp'}, use_global_device_ids=true, to_apply=%add.3 | all-reduce | flops 3072 | bytes 12288
  91.2 33.0 %all-gather.6.cloned.1.call-done = bf16[768,2304]{1,0:T(8,128)(2,1)} async-done(((bf16[96,2304]{1,0:T(8,128)(2,1)}), bf16[768,2304]{1,0:T(8,128)(2,1)}) %all-gather.6.cloned.1.call-update) | async-done | bytes 3538960 | tf_op jit(solution)/shard_map/all_gather | solution.py:92
  134.9 9.6 copy.106
  149.6 9.6 copy.109
  159.2 9.9 fusion.75
  190.3 56.4 %all-gather.12.cloned.1.call-done = bf16[768,3072]{1,0:T(8,128)(2,1)} async-done(((bf16[96,3072]{1,0:T(8,128)(2,1)}), bf16[768,3072]{1,0:T(8,128)(2,1)}) %all-gather.12.cloned.1.call-update) | async-done | bytes 4718608 | tf_op jit(solution)/shard_map/all_gather | solution.py:95
  246.6 11.6 %multiply_convert_fusion.1 = (bf16[256,3072]{1,0:T(8,128)(2,1)}, f32[256,3072]{1,0:T(8,128)}, f32[256,3072]{1,0:T(8,128)}) fusion(bf16[768,3072]{1,0:T(8,128)(2,1)} %all-gather.12.cloned.1.call-done, f32[256,768]{1,0:T(8,128)} %copy-done.15, f32[768]{0:T(1024)} %convert_element_type.172, f32[768]{0:T(1024)} %convert_element_type.171, ...), kind=kOutput, calls=%fused_computation.34 | convolution fusion | flops 1260060672 | bytes 13377536 | tf_op jit(solution)/shard_map/dot_general | solution.py:218
  258.2 68.5 %all-gather.14.cloned.1.call-done = bf16[3072,768]{1,0:T(8,128)(2,1)} async-done(((bf16[384,768]{1,0:T(8,128)(2,1)}), bf16[3072,768]{1,0:T(8,128)(2,1)}) %all-gather.14.cloned.1.call-update) | async-done | bytes 4718608 | tf_op jit(solution)/shard_map/all_gather | solution.py:96
  359.0 7.2 fusion.73
  366.2 7.7 subtract_convert_fusion.1
  405.6 8.2 copy.144
  429.6 26.1 %reduce-scatter.19.cloned.1.call-done = f32[96,768]{1,0:T(8,128)} async-done(((f32[768,768]{1,0:T(8,128)}), f32[96,768]{1,0:T(8,128)}) %reduce-scatter.19.cloned.1.call-update) | async-done | bytes 294928 | tf_op jit(solution)/shard_map/reduce_scatter | solution.py:305
  457.4 69.9 %reduce-scatter.15.cloned.1.call-done = f32[96,768]{1,0:T(8,128)} async-done(((f32[768,768]{1,0:T(8,128)}), f32[96,768]{1,0:T(8,128)}) %reduce-scatter.15.cloned.1.call-update) | async-done | bytes 294928 | tf_op jit(solution)/shard_map/reduce_scatter | solution.py:304
  528.9 130.1 %reduce-scatter.31.cloned.1.call-done = f32[96,2304]{1,0:T(8,128)} async-done(((f32[768,2304]{1,0:T(8,128)}), f32[96,2304]{1,0:T(8,128)}) %reduce-scatter.31.cloned.1.call-update) | async-done | bytes 884752
  661.9 163.6 %reduce-scatter.27.cloned.1.call-done = f32[384,768]{1,0:T(8,128)} async-done(((f32[3072,768]{1,0:T(8,128)}), f32[384,768]{1,0:T(8,128)}) %reduce-scatter.27.cloned.1.call-update) | async-done | bytes 1179664 | tf_op jit(solution)/shard_map/reduce_scatter | solution.py:307
  827.7 164.2 %reduce-scatter.23.cloned.1.call-done = f32[96,3072]{1,0:T(8,128)} async-done(((f32[768,3072]{1,0:T(8,128)}), f32[96,3072]{1,0:T(8,128)}) %reduce-scatter.23.cloned.1.call-update) | async-done | bytes 1179664 | tf_op jit(solution)/shard_map/reduce_scatter | solution.py:306
  995.3 39.7 %all-reduce.16 = (f32[1]{0:T(128)}, f32[1]{0:T(128)}, f32[1]{0:T(128)}) all-reduce(f32[1]{0:T(128)} %bitcast.50, f32[1]{0:T(128)} %bitcast.49, f32[1]{0:T(128)} %bitcast.48), channel_id=1, replica_groups=mesh['dp'=8,'rep'=4] {'dp','rep'}, use_global_device_ids=true, to_apply=%region_18.19 | all-reduce | flops 3 | bytes 24 | tf_op jit(solution)/shard_map/psum | solution.py:224
  1035.1 36.8 %all-reduce.17 = (bf16[768]{0:T(1024)(128)(2,1)S(1)}, bf16[768]{0:T(1024)(128)(2,1)S(1)}, bf16[768]{0:T(1024)(128)(2,1)S(1)}, bf16[768]{0:T(1024)(128)(2,1)S(1)}) all-reduce(f32[768]{0:T(1024)S(1)} %copy-done.58, f32[768]{0:T(1024)S(1)} %copy-done.59, f32[768]{0:T(1024)S(1)} %copy-done.48, ...), channel_id=8, replica_groups=mesh['dp'=8,'rep'=4] {'dp'}, use_global_device_ids=true, to_apply=%region_26.27.clone | all-reduce | flops 3072 | bytes 18432
  1093.4 16.1 %reduce-scatter.25.cloned.1.call-done = bf16[24,3072]{1,0:T(8,128)(2,1)} async-done(((bf16[96,3072]{1,0:T(8,128)(2,1)}), bf16[24,3072]{1,0:T(8,128)(2,1)}) %reduce-scatter.25.cloned.1.call-update) | async-done | bytes 147472 | tf_op jit(solution)/shard_map/reduce_scatter | solution.py:344
  (293 shorter events, 167.9 us)
Async XLA Ops:
  7.3 82.2 %all-gather.8.cloned.1.call-start = ((), (), s32[]{:S(2)}) async-start(), calls=%async_computation.11 | async-start | bytes 1327104 | tf_op jit(solution)/shard_map/all_gather | solution.py:94
  15.8 108.4 %all-gather.6.cloned.1.call-start = ((), (), s32[]{:S(2)}) async-start(), calls=%async_computation.10 | async-start | bytes 3981312 | tf_op jit(solution)/shard_map/all_gather | solution.py:92
  23.8 162.1 %all-gather.10.cloned.1.call-start = ((), (), s32[]{:S(2)}) async-start(), calls=%async_computation.12 | async-start | bytes 1327104 | tf_op jit(solution)/shard_map/all_gather | solution.py:93
  30.7 215.9 %all-gather.12.cloned.1.call-start = ((), (), s32[]{:S(2)}) async-start(), calls=%async_computation.13 | async-start | bytes 5308416 | tf_op jit(solution)/shard_map/all_gather | solution.py:95
  39.6 84.6 %copy-start.30 = (bf16[256,768]{1,0:T(8,128)(2,1)S(1)}, bf16[256,768]{1,0:T(8,128)(2,1)}, u32[]{:S(2)}) copy-start(bf16[256,768]{1,0:T(8,128)(2,1)} %param.13) | copy-start | bytes 1179652
  39.6 287.1 %all-gather.14.cloned.1.call-start = ((), (), s32[]{:S(2)}) async-start(), calls=%async_computation.14 | async-start | bytes 5308416 | tf_op jit(solution)/shard_map/all_gather | solution.py:96
  49.3 406.4 %reduce-scatter.19.cloned.1.call-start = ((), (), s32[]{:S(2)}) async-start(), calls=%async_computation.17 | async-start | bytes 2654208 | tf_op jit(solution)/shard_map/reduce_scatter | solution.py:305
  50.8 118.2 %copy-start.18 = (f32[256,2,192]{0,2,1:T(8,128)}, f32[256,2,192]{0,2,1:T(8,128)S(1)}, u32[]{:S(2)}) copy-start(f32[256,2,192]{0,2,1:T(8,128)S(1)} %get-tuple-element.205) | copy-start | bytes 1179652
  52.6 122.7 %copy-start.26 = (bf16[2,1,256,192]{2,3,1,0:T(8,128)(2,1)}, bf16[2,1,256,192]{2,3,1,0:T(8,128)(2,1)S(1)}, u32[]{:S(2)}) copy-start(bf16[2,1,256,192]{2,3,1,0:T(8,128)(2,1)S(1)} %get-tuple-element.202) | copy-start | bytes 589828
  52.6 122.7 %copy-start.28 = (bf16[2,1,256,192]{2,3,1,0:T(8,128)(2,1)}, bf16[2,1,256,192]{2,3,1,0:T(8,128)(2,1)S(1)}, u32[]{:S(2)}) copy-start(bf16[2,1,256,192]{2,3,1,0:T(8,128)(2,1)S(1)} %get-tuple-element.203) | copy-start | bytes 589828
  181.8 162.9 %copy-start = (f32[12,256,256]{1,2,0:T(8,128)}, f32[12,256,256]{1,2,0:T(8,128)S(1)}, u32[]{:S(2)}) copy-start(f32[12,256,256]{1,2,0:T(8,128)S(1)} %get-tuple-element.213) | copy-start | bytes 9437188
  388.4 138.9 %reduce-scatter.15.cloned.1.call-start = ((), (), s32[]{:S(2)}) async-start(), calls=%async_computation.15 | async-start | bytes 2654208 | tf_op jit(solution)/shard_map/reduce_scatter | solution.py:304
  391.4 267.6 %reduce-scatter.31.cloned.1.call-start = ((), (), s32[]{:S(2)}) async-start(), calls=%async_computation.23 | async-start | bytes 7962624
  413.8 411.6 %reduce-scatter.27.cloned.1.call-start = ((), (), s32[]{:S(2)}) async-start(), calls=%async_computation.21 | async-start | bytes 10616832 | tf_op jit(solution)/shard_map/reduce_scatter | solution.py:307
  421.8 570.1 %reduce-scatter.23.cloned.1.call-start = ((), (), s32[]{:S(2)}) async-start(), calls=%async_computation.19 | async-start | bytes 10616832 | tf_op jit(solution)/shard_map/reduce_scatter | solution.py:306
  429.5 657.2 %reduce-scatter.21.cloned.1.call-start = ((), (), s32[]{:S(2)}) async-start(), calls=%async_computation.18 | async-start | bytes 184320 | tf_op jit(solution)/shard_map/reduce_scatter | solution.py:341
  457.3 630.8 %reduce-scatter.17.cloned.1.call-start = ((), (), s32[]{:S(2)}) async-start(), calls=%async_computation.16 | async-start | bytes 184320 | tf_op jit(solution)/shard_map/reduce_scatter | solution.py:338
  528.9 560.7 %reduce-scatter.33.cloned.1.call-start = ((), (), s32[]{:S(2)}) async-start(), calls=%async_computation.24 | async-start | bytes 552960
  660.5 374.6 %copy-start.48 = (f32[768]{0:T(1024)S(1)}, f32[768]{0:T(1024)}, u32[]{:S(2)}) copy-start(f32[768]{0:T(1024)} %get-tuple-element.149) | copy-start | bytes 9220
  660.5 374.5 %copy-start.49 = (f32[768]{0:T(1024)S(1)}, f32[768]{0:T(1024)}, u32[]{:S(2)}) copy-start(f32[768]{0:T(1024)} %get-tuple-element.155) | copy-start | bytes 9220
  660.5 374.5 %copy-start.58 = (f32[768]{0:T(1024)S(1)}, f32[768]{0:T(1024)}, u32[]{:S(2)}) copy-start(f32[768]{0:T(1024)} %get-tuple-element.147) | copy-start | bytes 9220
  660.5 374.5 %copy-start.59 = (f32[768]{0:T(1024)S(1)}, f32[768]{0:T(1024)}, u32[]{:S(2)}) copy-start(f32[768]{0:T(1024)} %get-tuple-element.152) | copy-start | bytes 9220
  661.6 430.2 %reduce-scatter.29.cloned.1.call-start = ((), (), s32[]{:S(2)}) async-start(), calls=%async_computation.22 | async-start | bytes 737280 | tf_op jit(solution)/shard_map/reduce_scatter | solution.py:347
  827.6 281.9 %reduce-scatter.25.cloned.1.call-start = ((), (), s32[]{:S(2)}) async-start(), calls=%async_computation.20 | async-start | bytes 737280 | tf_op jit(solution)/shard_map/reduce_scatter | solution.py:344
  (66 other events, 653.1 us)
Sparse Core Ops, SparseCore 0:
  15.9 41.4 all-gather.7
  59.6 64.5 all-gather.5
  126.3 39.5 all-gather.9
  168.0 78.6 all-gather.11
  248.7 78.0 all-gather.13
  388.5 67.1 reduce-scatter.18
  459.2 68.0 reduce-scatter.14
  530.9 128.0 reduce-scatter.30
  663.0 162.3 reduce-scatter.26
  829.3 162.5 reduce-scatter.22
  995.0 18.7 reduce-scatter.20
  1016.8 19.6 reduce-scatter.16
  1039.2 21.1 reduce-scatter.32
  1062.8 22.0 reduce-scatter.28
  1087.4 22.0 reduce-scatter.24
where the time goes:
time: 1120 us
  waiting for transfers between devices  728 us (65%)
  blocking collectives  153 us (14%)
  matrix products  95 us (8%)
  local copies, waits for them, and re-layouts  74.3 us (7%)
  other arithmetic  49.3 us (4%)
  between operations  17.8 us (2%)
    reduce_scatter x1, waiting for transfers between devices, body(): lax.psum_scatter(grad_w_up, 'dp', scatter_dimension=0, tiled=True)  164 us
    reduce_scatter x1, waiting for transfers between devices, body(): lax.psum_scatter(grad_w_down, 'dp', scatter_dimension=0, tiled=True)  164 us
    unnamed x17, waiting for transfers between devices  130 us
    unnamed x4, blocking collectives  71.4 us
    reduce_scatter x1, waiting for transfers between devices, body(): lax.psum_scatter(grad_w_out, 'dp', scatter_dimension=0, tiled=True)  69.9 us
    all_gather x1, waiting for transfers between devices, fetch_weights(): lax.all_gather(in_down, 'dp', axis=0, tiled=True)  68.5 us
    all_gather x1, waiting for transfers between devices, fetch_weights(): lax.all_gather(in_up, 'dp', axis=0, tiled=True)  56.4 us
    psum x1, blocking collectives, body(): lax.psum((jnp.sum(tokens_f * tokens_f), jnp.sum(attn_out * attn_out), jnp...  39.7 us
  transfers between devices with their start and end apart: 15, of which 9 were waited for; matrix products, arithmetic and copies ran while one was open for 13% of the time, Pallas kernels for 0%

commit v1 on v0

--- a/solution.py
+++ b/solution.py
@@ -74,30 +74,24 @@
 
 
 def fetch_weights(w_qkv, w_out, w_pos, w_up, w_down, gain_attn, bias_attn, gain_ffn, bias_ffn):
-    inner = (
-        lax.all_gather(w_qkv, "rep", axis=0, tiled=True),
-        lax.all_gather(w_out, "rep", axis=0, tiled=True),
-        lax.all_gather(w_pos, "rep", axis=0, tiled=True),
-        lax.all_gather(w_up, "rep", axis=0, tiled=True),
-        lax.all_gather(w_down, "rep", axis=0, tiled=True),
-        lax.all_gather(gain_attn, "rep", axis=0, tiled=True),
-        lax.all_gather(bias_attn, "rep", axis=0, tiled=True),
-        lax.all_gather(gain_ffn, "rep", axis=0, tiled=True),
-        lax.all_gather(bias_ffn, "rep", axis=0, tiled=True),
-    )
-    in_qkv, in_out, in_pos, in_up, in_down, in_gain_attn, in_bias_attn, in_gain_ffn, in_bias_ffn = (
-        inner
-    )
+    axes = ("dp", "rep")
+    width = w_out.shape[1]
+    first = jnp.concatenate([w_qkv, w_pos, w_out], axis=1)
+    first = lax.all_gather(first, axes, axis=0, tiled=True)
+    wide = lax.all_gather(w_up, axes, axis=0, tiled=True)
+    deep = lax.all_gather(w_down, axes, axis=0, tiled=True)
+    small = jnp.stack([gain_attn, bias_attn, gain_ffn, bias_ffn], axis=1)
+    small = lax.all_gather(small, axes, axis=0, tiled=True)
     return (
-        lax.all_gather(in_qkv, "dp", axis=0, tiled=True),
-        lax.all_gather(in_out, "dp", axis=0, tiled=True),
-        lax.all_gather(in_pos, "dp", axis=0, tiled=True),
-        lax.all_gather(in_up, "dp", axis=0, tiled=True),
-        lax.all_gather(in_down, "dp", axis=0, tiled=True),
-        lax.all_gather(in_gain_attn, "dp", axis=0, tiled=True),
-        lax.all_gather(in_bias_attn, "dp", axis=0, tiled=True),
-        lax.all_gather(in_gain_ffn, "dp", axis=0, tiled=True),
-        lax.all_gather(in_bias_ffn, "dp", axis=0, tiled=True),
+        first[:, : 3 * width],
+        first[:, 4 * width :],
+        first[:, 3 * width : 4 * width],
+        wide,
+        deep,
+        small[:, 0],
+        small[:, 1],
+        small[:, 2],
+        small[:, 3],
     )
 
 
@@ -231,17 +225,8 @@
     )
     entry_count = tok_count * width * lax.axis_size("dp") * lax.axis_size("rep")
     rms_values = jnp.sqrt(jnp.stack([sum_tokens, sum_attn, sum_resid]) / entry_count)
-    (
-        back_qkv,
-        back_out,
-        back_pos,
-        back_up,
-        back_down,
-        back_gain_attn,
-        back_bias_attn,
-        back_gain_ffn,
-        back_bias_ffn,
-    ) = fetch_weights(w_qkv, w_out, w_pos, w_up, w_down, gain_attn, bias_attn, gain_ffn, bias_ffn)
+    back_qkv, back_out, back_pos, back_up, back_down = full_qkv, full_out, full_pos, full_up, full_down
+    back_gain_attn, back_gain_ffn = full_gain_attn, full_gain_ffn
     back_pos_heads = back_pos.reshape(pos_width, HEADS, head_dim)
     grad_resid_two, grad_gain_ffn, grad_bias_ffn = norm_backward(
         cotangent.astype(jnp.float32),
@@ -299,67 +284,27 @@
     grad_tokens = grad_resid_one + jnp.einsum(
         "te,de->td", grad_qkv, back_qkv, preferred_element_type=jnp.float32
     )
-    outer = (
-        lax.psum_scatter(grad_w_qkv, "dp", scatter_dimension=0, tiled=True),
-        lax.psum_scatter(grad_w_out, "dp", scatter_dimension=0, tiled=True),
-        lax.psum_scatter(grad_w_pos, "dp", scatter_dimension=0, tiled=True),
-        lax.psum_scatter(grad_w_up, "dp", scatter_dimension=0, tiled=True),
-        lax.psum_scatter(grad_w_down, "dp", scatter_dimension=0, tiled=True),
-        lax.psum_scatter(grad_gain_attn, "dp", scatter_dimension=0, tiled=True),
-        lax.psum_scatter(grad_bias_attn, "dp", scatter_dimension=0, tiled=True),
-        lax.psum_scatter(grad_gain_ffn, "dp", scatter_dimension=0, tiled=True),
-        lax.psum_scatter(grad_bias_ffn, "dp", scatter_dimension=0, tiled=True),
-    )
-    (
-        part_qkv,
-        part_out,
-        part_pos,
-        part_up,
-        part_down,
-        part_gain_attn,
-        part_bias_attn,
-        part_gain_ffn,
-        part_bias_ffn,
-    ) = outer
-    (
-        sum_qkv,
-        sum_out,
-        sum_pos,
-        sum_up,
-        sum_down,
-        sum_gain_attn,
-        sum_bias_attn,
-        sum_gain_ffn,
-        sum_bias_ffn,
-    ) = (
-        lax.psum_scatter(
-            part_qkv.astype(jnp.bfloat16), "rep", scatter_dimension=0, tiled=True
-        ).astype(jnp.float32),
-        lax.psum_scatter(
-            part_out.astype(jnp.bfloat16), "rep", scatter_dimension=0, tiled=True
-        ).astype(jnp.float32),
-        lax.psum_scatter(
-            part_pos.astype(jnp.bfloat16), "rep", scatter_dimension=0, tiled=True
-        ).astype(jnp.float32),
-        lax.psum_scatter(
-            part_up.astype(jnp.bfloat16), "rep", scatter_dimension=0, tiled=True
-        ).astype(jnp.float32),
-        lax.psum_scatter(
-            part_down.astype(jnp.bfloat16), "rep", scatter_dimension=0, tiled=True
-        ).astype(jnp.float32),
-        lax.psum_scatter(
-            part_gain_attn.astype(jnp.bfloat16), "rep", scatter_dimension=0, tiled=True
-        ).astype(jnp.float32),
-        lax.psum_scatter(
-            part_bias_attn.astype(jnp.bfloat16), "rep", scatter_dimension=0, tiled=True
-        ).astype(jnp.float32),
-        lax.psum_scatter(
-            part_gain_ffn.astype(jnp.bfloat16), "rep", scatter_dimension=0, tiled=True
-        ).astype(jnp.float32),
-        lax.psum_scatter(
-            part_bias_ffn.astype(jnp.bfloat16), "rep", scatter_dimension=0, tiled=True
-        ).astype(jnp.float32),
-    )
+    axes = ("dp", "rep")
+
+    def scatter_sum(values):
+        return lax.psum_scatter(values, axes, scatter_dimension=0, tiled=True).astype(jnp.float32)
+
+    low = jnp.bfloat16
+    sum_down = scatter_sum(grad_w_down.astype(low))
+    sum_up = scatter_sum(grad_w_up.astype(low))
+    sum_first = scatter_sum(
+        jnp.concatenate([grad_w_qkv.astype(low), grad_w_pos.astype(low), grad_w_out.astype(low)], axis=1)
+    )
+    sum_qkv = sum_first[:, : 3 * width]
+    sum_pos = sum_first[:, 3 * width : 4 * width]
+    sum_out = sum_first[:, 4 * width :]
+    sum_small = lax.psum_scatter(
+        jnp.stack([grad_gain_attn, grad_bias_attn, grad_gain_ffn, grad_bias_ffn], axis=1),
+        axes,
+        scatter_dimension=0,
+        tiled=True,
+    )
+    sum_gain_attn, sum_bias_attn, sum_gain_ffn, sum_bias_ffn = [sum_small[:, i] for i in range(4)]
     return (
         output.astype(jnp.bfloat16),
         grad_tokens,

time: 1120 us -> 578 us (0.52)
  waiting for transfers between devices: 728 us -> 308 us
  blocking collectives: 153 us -> 83.8 us
  local copies, waits for them, and re-layouts: 74.3 us -> 45.5 us
  matrix products: 95 us -> 71.5 us
    reduce_scatter x8 -> x2, waiting for transfers between devices: 440 us -> 89 us  [scatter_sum(): lax.psum_scatter(values, axes, scatter_dimension=0, tiled=True)]
    unnamed x4 -> x0, blocking collectives: 71.4 us -> none
    all_gather x5 -> x3, waiting for transfers between devices: 158 us -> 102 us  [the longest x1 53.6 us: fetch_weights(): deep = lax.all_gather(w_down, axes, axis=0, tiled=True)]
    transpose x2 -> x0, local copies, waits for them, and re-layouts: 19.2 us -> none  [the longest x1 9.62 us: body(): jnp.einsum('thd,phd->thp', query, pos_weights, preferred_element_type=jnp...]
    convert_element_type x15 -> x2, other arithmetic: 17.8 us -> 3.29 us  [scatter_sum(): lax.psum_scatter(values, axes, scatter_dimension=0, tiled=True)]
    unnamed x17 -> x7, waiting for transfers between devices: 130 us -> 117 us
    unnamed x176 -> x107, local copies, waits for them, and re-layouts: 25.4 us -> 23.5 us
    all_gather x5 -> x1, blocking collectives: 41.7 us -> 43.3 us  [fetch_weights(): small = lax.all_gather(small, axes, axis=0, tiled=True)]
  transfers between devices with their start and end apart: 15 -> 6, of which waited for: 9 -> 5; matrix products, arithmetic and copies ran while one was open for 13% -> 24% of each run, Pallas kernels for 0% -> 0%
where the time goes in v1:
time: 578 us; the launch traced here: 571 us
  waiting for transfers between devices  308 us (53%)
  blocking collectives  83.8 us (14%)
  matrix products  71.5 us (12%)
  other arithmetic  45.8 us (8%)
  local copies, waits for them, and re-layouts  45.5 us (8%)
  between operations  15 us (3%)
    unnamed x7, waiting for transfers between devices  117 us
    reduce_scatter x2, waiting for transfers between devices, scatter_sum(): lax.psum_scatter(values, axes, scatter_dimension=0, tiled=True)  89 us
    all_gather x1, waiting for transfers between devices, fetch_weights(): deep = lax.all_gather(w_down, axes, axis=0, tiled=True)  53.6 us
    all_gather x1, blocking collectives, fetch_weights(): small = lax.all_gather(small, axes, axis=0, tiled=True)  43.3 us
    psum x1, blocking collectives, body(): lax.psum((jnp.sum(tokens_f * tokens_f), jnp.sum(attn_out * attn_out), jnp...  40.5 us
    all_gather x1, waiting for transfers between devices, fetch_weights(): wide = lax.all_gather(w_up, axes, axis=0, tiled=True)  29 us
    unnamed x107, local copies, waits for them, and re-layouts  23.5 us
    all_gather x1, waiting for transfers between devices, fetch_weights(): first = lax.all_gather(first, axes, axis=0, tiled=True)  19.7 us
  transfers between devices with their start and end apart: 6, of which 5 were waited for; matrix products, arithmetic and copies ran while one was open for 24% of the time, Pallas kernels for 0%

profile of v1, /device:TPU:0, one launch (start us, length us, event | category | flops | bytes accessed | tf_op | source)
XLA Modules:
  0.0 571.1 jit_solution(10890113409451673832)
XLA Ops:
  13.5 43.3 %all-gather = bf16[32,24,4]{1,2,0:T(4,128)(2,1)S(1)} all-gather(bf16[1,24,4]{1,2,0:T(4,128)(2,1)S(1)} %maximum_bitcast_fusion), channel_id=1, replica_groups=mesh['dp'=8,'rep'=4] {'dp','rep'}, dimensions={0}, use_global_device_ids=true | all-gather | bytes 6336 | tf_op jit(solution)/shard_map/all_gather | solution.py:84
  62.2 19.7 %all-gather.5.cloned.1.call-done = bf16[768,3840]{1,0:T(8,128)(2,1)} async-done(((bf16[24,3840]{1,0:T(8,128)(2,1)}), bf16[768,3840]{1,0:T(8,128)(2,1)}) %all-gather.5.cloned.1.call-update) | async-done | bytes 5898256 | tf_op jit(solution)/shard_map/all_gather | solution.py:80
  83.9 3.6 convolution_convert_fusion.3
  88.9 2.7 fusion.62
  91.6 6.9 %fusion.86 = (f32[256,12,2,1,192]{0,4,3,2,1:T(8,128)}, f32[256,12,2,1,192]{0,4,3,2,1:T(8,128)}, f32[256,12,2,1,192]{0,4,3,2,1:T(8,128)}, f32[256,12,2,1,192]{0,4,3,2,1:T(8,128)}) fusion(f32[256,12,2,2,192]{0,4,3,2,1:T(8,128)S(1)} %bitcast.153, f32[256,12,2,2,192]{0,4,3,2,1:T(8,128)S(1)} %bitcast.152), kind=kLoop, calls=%fused_computation.165 | loop fusion | bytes 37748736 | tf_op jit(solution)/shard_map/slice | solution.py:34
  98.5 8.5 %subtract_convert_fusion.2 = (bf16[256,12,2,1,192]{0,4,3,1,2:T(8,128)(2,1)S(1)}, bf16[256,12,2,1,192]{0,4,3,1,2:T(8,128)(2,1)S(1)}, bf16[256,12,2,1,192]{0,4,3,1...) fusion(f32[256,12,2,1,192]{0,4,3,2,1:T(8,128)} %get-tuple-element.181, f32[256,12,2,1,192]{0,4,3,2,1:T(8,128)} %get-tuple-element.180, ...), kind=kLoop, calls=%fused_computation.22 | loop fusion | flops 18874368 | bytes 29097984 | tf_op jit(solution)/shard_map/convert.17
  118.4 29.0 %all-gather.7.cloned.1.call-done = bf16[768,3072]{1,0:T(8,128)(2,1)} async-done(((bf16[24,3072]{1,0:T(8,128)(2,1)}), bf16[768,3072]{1,0:T(8,128)(2,1)}) %all-gather.7.cloned.1.call-update) | async-done | bytes 4718608 | tf_op jit(solution)/shard_map/all_gather | solution.py:81
  147.4 11.7 %multiply_convert_fusion.1 = (bf16[256,3072]{1,0:T(8,128)(2,1)}, f32[256,3072]{1,0:T(8,128)}, f32[256,3072]{1,0:T(8,128)}) fusion(bf16[768,3072]{1,0:T(8,128)(2,1)} %all-gather.7.cloned.1.call-done, f32[256,768]{1,0:T(8,128)} %copy-done.8, f32[768]{0:T(1024)S(1)} %get-tuple-element.158, f32[768]{0:T(1024)S(1)} %get-tuple-element.159, ...), kind=kOutput, calls=%fused_computation.36 | convolution fusion | flops 1260060672 | bytes 13377536 | tf_op jit(solution)/shard_map/dot_general | solution.py:212
  159.1 53.6 %all-gather.9.cloned.1.call-done = bf16[3072,768]{1,0:T(8,128)(2,1)} async-done(((bf16[96,768]{1,0:T(8,128)(2,1)}), bf16[3072,768]{1,0:T(8,128)(2,1)}) %all-gather.9.cloned.1.call-update) | async-done | bytes 4718608 | tf_op jit(solution)/shard_map/all_gather | solution.py:82
  212.8 4.5 fusion.91
  220.4 3.8 convolution_convert_fusion
  226.7 6.9 %add_convert_fusion.4 = bf16[256,3072]{1,0:T(8,128)(2,1)S(1)} fusion(f32[256,3072]{1,0:T(8,128)} %get-tuple-element.165, f32[256,3072]{1,0:T(8,128)} %get-tuple-element.205, bf16[3072,768]{1,0:T(8,128)(2,1)} %all-gather.9.cloned.1.call-done, bf16[256,768]{1,0:T(8,128)(2,1)} %param.16, f32[256,768]{1,0:T(8,128)} %copy-done.10, f32[256]{0:T(256)} %copy-done.40, ...), kind=kOutput, calls=%fused_computation.35 | convolution fusion | flops 1220739072 | bytes 13769728 | tf_op jit(solution)/shard_map/td,fd->tf/dot_general | solution.py:239
  233.7 5.6 multiply_reduce_fusion.1
  245.9 5.5 convolution_convert_fusion.1
  253.3 2.7 multiply_convert_fusion
  257.4 4.9 fusion.85
  264.0 4.7 fusion.84
  268.7 8.7 %subtract_convert_fusion.1 = (bf16[256,12,2,1,192]{0,4,3,1,2:T(8,128)(2,1)S(1)}, bf16[256,12,2,1,192]{0,4,3,1,2:T(8,128)(2,1)S(1)}, bf16[256,12,2,1,192]{0,4,3,1,2:T(8,128)(2,1)S(1)}, bf16[256,12,2,1,192]{0,4,3,1,2:T(8,128)(2,1)}) fusion(f32[256,12,2,1,192]{0,4,3,2,1:T(8,128)} %get-tuple-element.177, f32[256,12,2,1,192]{0,4,3,2,1:T(8,128)} %get-tuple-element.176, ...), kind=kLoop, calls=%fused_computation.18 | loop fusion | flops 18874368 | bytes 29097984 | tf_op jit(solution)/shard_map/convert.15
  291.8 3.1 pad_maximum_fusion
  294.9 8.5 %copy.136 = bf16[768,3840]{1,0:T(8,128)(2,1)} copy(bf16[768,3840]{0,1:T(8,128)(2,1)} %pad_maximum_fusion) | data formatting | bytes 11796480
  304.2 40.5 %all-reduce.1 = (f32[1]{0:T(128)}, f32[1]{0:T(128)}, f32[1]{0:T(128)}, f32[768,4]{0,1:T(4,128)S(1)}) all-reduce(f32[1]{0:T(128)} %bitcast.55, f32[1]{0:T(128)} %bitcast.54, f32[1]{0:T(128)} %bitcast.53, f32[768,4]{0,1:T(4,128)S(1)} %pad_maximum_fusion.5), channel_id=1, replica_groups=mesh['dp'=8,'rep'=4] {'dp','rep'}, use_global_device_ids=true, to_apply=%region_18.19 | all-reduce | flops 3075 | bytes 24600 | tf_op jit(solution)/shard_map/psum | solution.py:218
  347.9 4.1 fusion.30
  353.6 89.0 %reduce-scatter.7.cloned.1.call-done = bf16[24,3072]{1,0:T(8,128)(2,1)} async-done(((bf16[768,3072]{1,0:T(8,128)(2,1)}), bf16[24,3072]{1,0:T(8,128)(2,1)}) %reduce-scatter.7.cloned.1.call-update) | async-done | bytes 147472 | tf_op jit(solution)/shard_map/reduce_scatter | solution.py:290
  444.2 115.7 %reduce-scatter.11.cloned.1.call-done = bf16[24,3840]{1,0:T(8,128)(2,1)} async-done(((bf16[768,3840]{1,0:T(8,128)(2,1)}), bf16[24,3840]{1,0:T(8,128)(2,1)}) %reduce-scatter.11.cloned.1.call-update) | async-done | bytes 184336
  (186 shorter events, 68.9 us)
Async XLA Ops:
  7.2 74.7 %all-gather.5.cloned.1.call-start = ((), (), s32[]{:S(2)}) async-start(), calls=%async_computation.3 | async-start | bytes 6082560 | tf_op jit(solution)/shard_map/all_gather | solution.py:80
  8.9 138.6 %all-gather.7.cloned.1.call-start = ((), (), s32[]{:S(2)}) async-start(), calls=%async_computation.4 | async-start | bytes 4866048 | tf_op jit(solution)/shard_map/all_gather | solution.py:81
  9.6 74.2 %copy-start.23 = (bf16[256,768]{1,0:T(8,128)(2,1)S(1)}, bf16[256,768]{1,0:T(8,128)(2,1)}, u32[]{:S(2)}) copy-start(bf16[256,768]{1,0:T(8,128)(2,1)} %param.13) | copy-start | bytes 1179652
  9.6 203.1 %all-gather.9.cloned.1.call-start = ((), (), s32[]{:S(2)}) async-start(), calls=%async_computation.5 | async-start | bytes 4866048 | tf_op jit(solution)/shard_map/all_gather | solution.py:82
  10.4 341.6 %reduce-scatter.9.cloned.1.call-start = ((), (), s32[]{:S(2)}) async-start(), calls=%async_computation.7 | async-start | bytes 4866048 | tf_op jit(solution)/shard_map/reduce_scatter | solution.py:290
  59.8 153.0 %copy-start.29 = (f32[768]{0:T(1024)}, f32[768]{0:T(1024)S(1)}, u32[]{:S(2)}) copy-start(f32[768]{0:T(1024)S(1)} %get-tuple-element.158) | copy-start | bytes 9220
  59.8 179.5 %copy-start.28 = (f32[768]{0:T(1024)}, f32[768]{0:T(1024)S(1)}, u32[]{:S(2)}) copy-start(f32[768]{0:T(1024)S(1)} %get-tuple-element.159) | copy-start | bytes 9220
  98.5 8.5 %copy-start.21 = (bf16[2,1,256,192]{2,3,1,0:T(8,128)(2,1)S(1)}, bf16[2,1,256,192]{2,3,1,0:T(8,128)(2,1)}, u32[]{:S(2)}) copy-start(bf16[2,1,256,192]{2,3,1,0:T(8,128)(2,1)} %get-tuple-element.193) | copy-start | bytes 589828
  98.5 8.5 %copy-start.22 = (bf16[2,1,256,192]{2,3,1,0:T(8,128)(2,1)S(1)}, bf16[2,1,256,192]{2,3,1,0:T(8,128)(2,1)}, u32[]{:S(2)}) copy-start(bf16[2,1,256,192]{2,3,1,0:T(8,128)(2,1)} %get-tuple-element.194) | copy-start | bytes 589828
  111.5 139.8 %copy-start = (f32[12,256,256]{1,2,0:T(8,128)}, f32[12,256,256]{1,2,0:T(8,128)S(1)}, u32[]{:S(2)}) copy-start(f32[12,256,256]{1,2,0:T(8,128)S(1)} %get-tuple-element.204) | copy-start | bytes 9437188
  113.0 4.9 copy-start.26
  116.7 122.7 %copy-start.33 = (f32[256]{0:T(256)}, f32[256]{0:T(256)S(1)}, u32[]{:S(2)}) copy-start(f32[256]{0:T(256)S(1)} %broadcast_multiply_fusion.7) | copy-start | bytes 3076
  212.8 4.8 copy-start.18
  212.8 4.8 copy-start.34
  224.3 218.3 %reduce-scatter.7.cloned.1.call-start = ((), (), s32[]{:S(2)}) async-start(), calls=%async_computation.6 | async-start | bytes 4866048 | tf_op jit(solution)/shard_map/reduce_scatter | solution.py:290
  226.6 7.0 %copy-start.9 = (f32[256,768]{1,0:T(8,128)S(1)}, f32[256,768]{1,0:T(8,128)}, u32[]{:S(2)}) copy-start(f32[256,768]{1,0:T(8,128)} %copy-done.8) | copy-start | bytes 2359300
  226.6 7.0 %copy-start.11 = (f32[256,768]{1,0:T(8,128)S(1)}, f32[256,768]{1,0:T(8,128)}, u32[]{:S(2)}) copy-start(f32[256,768]{1,0:T(8,128)} %copy-done.10) | copy-start | bytes 2359300
  226.7 7.0 %copy-start.19 = (bf16[256,768]{1,0:T(8,128)(2,1)S(1)}, bf16[256,768]{1,0:T(8,128)(2,1)}, u32[]{:S(2)}) copy-start(bf16[256,768]{1,0:T(8,128)(2,1)} %param.16) | copy-start | bytes 1179652
  226.7 7.0 %copy-start.37 = (f32[256]{0:T(256)S(1)}, f32[256]{0:T(256)}, u32[]{:S(2)}) copy-start(f32[256]{0:T(256)} %add_rsqrt_fusion.1) | copy-start | bytes 3076
  226.7 7.0 %copy-start.39 = (f32[256]{0:T(256)S(1)}, f32[256]{0:T(256)}, u32[]{:S(2)}) copy-start(f32[256]{0:T(256)} %copy-done.38) | copy-start | bytes 3076
  226.7 7.0 %copy-start.41 = (f32[256]{0:T(256)S(1)}, f32[256]{0:T(256)}, u32[]{:S(2)}) copy-start(f32[256]{0:T(256)} %copy-done.40) | copy-start | bytes 3076
  226.7 7.0 %copy-start.43 = (f32[256]{0:T(256)S(1)}, f32[256]{0:T(256)}, u32[]{:S(2)}) copy-start(f32[256]{0:T(256)} %copy-done.42) | copy-start | bytes 3076
  233.7 5.6 copy-start.20
  262.3 297.6 %reduce-scatter.11.cloned.1.call-start = ((), (), s32[]{:S(2)}) async-start(), calls=%async_computation.8 | async-start | bytes 6082560
  (33 other events, 61.5 us)
Sparse Core Ops, SparseCore 0:
  11.5 70.3 all-gather.4
  84.8 62.5 all-gather.6
  150.3 62.3 all-gather.8
  224.4 105.6 reduce-scatter.8
  336.3 106.1 reduce-scatter.6
  448.0 111.7 reduce-scatter.10
